TPU v7x, 32 devices: a whole 2x2x4 slice. The times are simulated.
32 devices in a mesh: pipe: 2 (over x), ctx: 8 (over z, core), tp: 2 (over y).
Axes of the slice: x: 2, y: 2, z: 4, core: 2. Of those that a mesh axis runs over, the one named last changes fastest.
Arguments:
- queries: bfloat16 [2, 512, 128, 128], P('pipe', 'ctx', 'tp'), may hold values from -10 to 10
- span_keys: bfloat16 [2, 512, 8, 128], P('pipe', 'ctx', 'tp'), may hold values from -6 to 6
- span_values: bfloat16 [2, 512, 8, 128], P('pipe', 'ctx', 'tp'), may hold values from -12 to 12
- cache_keys: bfloat16 [2, 256, 8, 128], P('pipe', 'ctx', 'tp'), may hold values from -6 to 6
- cache_values: bfloat16 [2, 256, 8, 128], P('pipe', 'ctx', 'tp'), may hold values from -6 to 6
- scale_exps: int32 [2, 16, 8, 2], P('pipe', 'ctx', 'tp'), may hold values from -3 to 1
- block_order: int32 [2, 16], P('pipe'), may hold values from 0 to 15, each once within a row
Outputs:
- handed: bfloat16 [2, 512, 128, 128], P('pipe', 'ctx', 'tp')
All inputs are finite; a program needn't handle non-finite values.
Results may differ from a plain program's by a relative error of at most 0.006.
Values may be sent and summed in bfloat16 or wider, within the bound.
A program may use at most 128 MiB of HBM per device.

v0:
```python
import jax
import jax.numpy as jnp
from jax import lax
from jax.sharding import PartitionSpec as P

CBLK = 16


def shifted(value, axis, steps):
    count = lax.axis_size(axis)
    pairs = [(source, (source + steps) % count) for source in range(count)]
    return lax.ppermute(value, axis, pairs)


def hadamard(order):
    rows = jnp.arange(order, dtype=jnp.int32)[:, None]
    cols = jnp.arange(order, dtype=jnp.int32)[None, :]
    common = jnp.zeros((order, order), jnp.int32)
    for bit in range(order.bit_length() - 1):
        common = common + (jnp.right_shift(rows, bit) & 1) * (jnp.right_shift(cols, bit) & 1)
    signs = 1.0 - 2.0 * (common % 2).astype(jnp.float32)
    return signs * (1.0 / order**0.5)


def table_lookup(table, slots):
    match = jnp.arange(table.shape[0], dtype=jnp.int32)[None, :] == slots[:, None]
    return jnp.sum(jnp.where(match, table[None, :], 0), axis=1)


def attend(carry, block, grouped, pos_query, order, half, cache_len, rows_dev):
    best, total, accum = carry
    keys = block[:, :, 0, :]
    vals = block[:, :, 1, :]
    count = block.shape[0]
    global_row = jnp.arange(count, dtype=jnp.int32)
    owner = global_row // rows_dev
    local = global_row % rows_dev
    offset = jnp.maximum(local - cache_len, 0)
    pos_key = table_lookup(order, 2 * owner + offset // half) * half + offset % half
    visible = (local < cache_len)[None, :] | (pos_key[None, :] <= pos_query[:, None])
    inv = 1.0 / grouped.shape[-1] ** 0.5
    score = jnp.einsum("tgqd,kgd->gqtk", grouped, keys, preferred_element_type=jnp.float32) * inv
    score = jnp.where(visible[None, None], score, -jnp.inf)
    best_new = jnp.max(score, axis=-1)
    safe = jnp.where(best_new == -jnp.inf, 0.0, best_new)
    expo = jnp.exp(score - safe[..., None])
    rescale = jnp.exp(best - safe)
    total = total * rescale + jnp.sum(expo, axis=-1)
    accum = accum * rescale[..., None] + jnp.einsum(
        "gqtk,kgd->gqtd", expo.astype(jnp.bfloat16), vals, preferred_element_type=jnp.float32
    )
    return (best_new, total, accum)


def on_device(queries, span_keys, span_values, cache_keys, cache_values, scale_exps, block_order):
    mine = lax.axis_index("ctx")
    tok_local = queries.shape[1]
    head_local = queries.shape[2]
    kv_local = span_keys.shape[2]
    width = queries.shape[3]
    cache_len = cache_keys.shape[1]
    half = tok_local // 2
    rows_dev = cache_len + tok_local
    grouped = queries[0].reshape(tok_local, kv_local, head_local // kv_local, width)
    order = block_order[0]
    factor = jnp.repeat(jnp.exp2(scale_exps[0].astype(jnp.float32)), CBLK, axis=0)
    keys_ctx = (cache_keys[0].astype(jnp.float32) * factor[:, :, 0:1]).astype(jnp.bfloat16)
    vals_ctx = (cache_values[0].astype(jnp.float32) * factor[:, :, 1:2]).astype(jnp.bfloat16)
    own_keys = jnp.concatenate([keys_ctx, span_keys[0]], axis=0)
    own_vals = jnp.concatenate([vals_ctx, span_values[0]], axis=0)
    own_block = jnp.stack([own_keys, own_vals], axis=2)
    index = jnp.arange(tok_local, dtype=jnp.int32)
    pos_query = table_lookup(order, 2 * mine + index // half) * half + index % half
    group_size = head_local // kv_local
    initial = (
        jnp.full((kv_local, group_size, tok_local), -jnp.inf, jnp.float32),
        jnp.zeros((kv_local, group_size, tok_local), jnp.float32),
        jnp.zeros((kv_local, group_size, tok_local, width), jnp.float32),
    )
    carry = attend(
        initial,
        lax.all_gather(own_block, "ctx", axis=0, tiled=True),
        grouped,
        pos_query,
        order,
        half,
        cache_len,
        rows_dev,
    )
    best, total, accum = carry
    mixed = accum / total[..., None]
    rotated = jnp.dot(mixed.reshape(-1, width), hadamard(width), precision=lax.Precision.HIGHEST)
    rotated = rotated.reshape(kv_local, group_size, tok_local, width).transpose(2, 0, 1, 3)
    result = rotated.reshape(1, tok_local, head_local, width).astype(jnp.bfloat16)
    return shifted(result, "pipe", 1)


def solution(mesh):
    placed = (
        P("pipe", "ctx", "tp", None),
        P("pipe", "ctx", "tp", None),
        P("pipe", "ctx", "tp", None),
        P("pipe", "ctx", "tp", None),
        P("pipe", "ctx", "tp", None),
        P("pipe", "ctx", "tp", None),
        P("pipe", None),
    )
    return jax.shard_map(
        on_device,
        mesh=mesh,
        in_specs=placed,
        out_specs=P("pipe", "ctx", "tp", None),
        check_vma=False,
    )
```

profile of v0, /device:TPU:0, one launch (start us, length us, event | category | flops | bytes accessed | tf_op | source)
XLA Modules:
  0.0 85.7 jit_solution(10235257192194648609)
XLA Ops:
  6.5 0.0 copy-start
  6.5 0.0 all-gather.2.cloned.1.call-start
  6.5 0.9 %copy.33 = bf16[1,64,4,128]{3,1,2,0:T(8,128)(2,1)S(1)} copy(bf16[1,64,4,128]{3,2,1,0:T(4,128)(2,1)} %param.9) | data formatting | bytes 131072 | tf_op args[2]
  7.5 0.7 exponential_bitcast_fusion
  8.2 0.1 copy.16
  8.3 0.1 broadcast_in_dim.66
  8.3 0.1 reshape.263
  8.4 0.9 %copy.34 = bf16[1,64,4,128]{3,1,2,0:T(8,128)(2,1)S(1)} copy(bf16[1,64,4,128]{3,2,1,0:T(4,128)(2,1)} %param.8) | data formatting | bytes 131072 | tf_op args[1]
  9.3 0.9 %fusion.23 = (bf16[32,4,128]{2,0,1:T(8,128)(2,1)S(1)}, bf16[32,4,128]{2,0,1:T(8,128)(2,1)S(1)}) fusion(bf16[1,32,4,128]{3,2,1,0:T(4,128)(2,1)} %param.11, f32[32,4]{0,1:T(4,128)S(1)} %get-tuple-element.8, f32[32,4]{0,1:T(4,128)S(1)} %get-tuple-element.7, bf16[1,32,4,128]{3,2,1,0:T(4,128)(2,1)} %param.10), kind=kLoop, calls=%fused_computation.32 | loop fusion | flops 98304 | bytes 132096 | tf_op jit(solution)/shard_map/convert_element_type | solution.py:68
  10.2 0.7 pad_maximum_fusion
  10.9 0.0 all-gather.2.cloned.1.call-update
  11.0 0.7 select_reduce_fusion.1
  11.8 0.7 select_reduce_fusion
  12.5 0.1 compare_or_fusion
  12.7 26.2 %all-gather.2.cloned.1.call-done = bf16[768,4,2,128]{3,0,1,2:T(8,128)(2,1)} async-done(((bf16[96,4,2,128]{3,0,1,2:T(8,128)(2,1)}), bf16[768,4,2,128]{3,0,1,2:T(8,128)(2,1)}) %all-gather.2.cloned.1.call-update) | async-done | bytes 1572880 | tf_op jit(solution)/shard_map/all_gather | solution.py:82
  38.9 0.0 copy-done
  38.9 0.0 copy-start.1
  38.9 4.0 %fusion.2 = (f32[4,16,64]{2,1,0:T(8,128)S(1)}, f32[4,768,64,16]{1,2,3,0:T(8,128)S(1)}) fusion(pred[64,768]{1,0:T(8,128)(4,1)S(1)} %compare_or_fusion, bf16[64,4,16,128]{3,2,1,0:T(8,128)(2,1)S(1)} %bitcast.57, bf16[768,4,2,128]{3,0,1,2:T(8,128)(2,1)} %all-gather.2.cloned.1.call-done), kind=kOutput, calls=%fused_computation.4 | convolution fusion | flops 814739456 | bytes 14483456 | tf_op jit(solution)/shard_map/tgqd,kgd->gqtk/dot_general | solution.py:42
  42.9 3.3 %fusion = f32[4,16,64]{2,1,0:T(8,128)S(1)} fusion(f32[4,768,64,16]{1,2,3,0:T(8,128)S(1)} %get-tuple-element.10, f32[4,16,64]{2,1,0:T(8,128)S(1)} %compare_select_fusion, pred[64,768]{1,0:T(8,128)(4,1)S(1)} %compare_or_fusion), kind=kLoop, calls=%fused_computation.2 | loop fusion | flops 12578816 | bytes 12664832 | tf_op jit(solution)/shard_map/reduce_sum | solution.py:48
  46.2 0.0 copy-done.1
  46.2 3.1 %fusion.3 = f32[4,16,64,128]{3,2,1,0:T(8,128)S(1)} fusion(f32[4,768,64,16]{1,2,3,0:T(8,128)S(1)} %get-tuple-element.10, f32[4,16,64]{2,1,0:T(8,128)S(1)} %compare_select_fusion, pred[64,768]{1,0:T(8,128)(4,1)S(1)} %compare_or_fusion, bf16[768,4,2,128]{3,0,1,2:T(8,128)(2,1)S(1)} %copy-done.1), kind=kOutput, calls=%fused_computation.5 | convolution fusion | flops 817889280 | bytes 15548416 | tf_op jit(solution)/shard_map/gqtk,kgd->gqtd/dot_general | solution.py:49
  49.3 2.5 %fusion.9 = bf16[4,16,64,128]{3,2,1,0:T(8,128)(2,1)S(1)} fusion(f32[4,16,64,128]{3,2,1,0:T(8,128)S(1)} %fusion.3, f32[4,16,64]{2,1,0:T(8,128)S(1)} %get-tuple-element.6, f32[4,16,64]{2,1,0:T(8,128)S(1)} %get-tuple-element.5, s32[128]{0:T(128)S(1)} %get-tuple-element.13, s32[128]{0:T(128)S(1)} %get-tuple-element.14, s32[128]{0:T(128)S(1)} %get-tuple-element.15, ...), kind=kOutput, calls=%fused_computation.10 | convolution fusion | flops 807337984 | bytes 3182080 | tf_op jit(solution)/shard_map/dot_general | solution.py:92
  51.8 0.7 copy.21
  52.5 1.5 %collective-permute-start = (bf16[1,64,64,128]{3,2,1,0:T(8,128)(2,1)S(1)}, bf16[1,64,64,128]{3,2,1,0:T(8,128)(2,1)S(1)}, u32[]{:S(2)}, u32[]{:S(2)}) collective-permute-start(bf16[1,64,64,128]{3,2,1,0:T(8,128)(2,1)S(1)} %copy.21), channel_id=1, source_target_pairs={{0,16},{16,0},{1,17},{17,1},{2,18},{18,2},{3,19},{19,3},{4,20},{20... | collective-permute-start | bytes 3145736 | tf_op jit(solution)/shard_map/ppermute | solution.py:12
  54.0 23.8 %collective-permute-done = bf16[1,64,64,128]{3,2,1,0:T(8,128)(2,1)S(1)} collective-permute-done((bf16[1,64,64,128]{3,2,1,0:T(8,128)(2,1)S(1)}, bf16[1,64,64,128]{3,2,1,0:T(8,128)(2,1)S(1)}, u32[]{:S(2)}, u32[]{:S(2)}) %collective-permute-start) | collective-permute-done | bytes 1048608 | tf_op jit(solution)/shard_map/ppermute | solution.py:12
  77.9 1.0 %copy.36 = bf16[1,64,64,128]{3,2,1,0:T(8,128)(2,1)} copy(bf16[1,64,64,128]{3,2,1,0:T(8,128)(2,1)S(1)} %collective-permute-done) | data formatting | bytes 2097152
  (14 shorter events, 0.1 us)
Async XLA Ops:
  6.5 32.3 %copy-start = (bf16[1,64,64,128]{3,2,1,0:T(8,128)(2,1)S(1)}, bf16[1,64,64,128]{3,2,1,0:T(8,128)(2,1)}, u32[]{:S(2)}) copy-start(bf16[1,64,64,128]{3,2,1,0:T(8,128)(2,1)} %param.7) | copy-start | bytes 3145732
  6.5 32.3 %all-gather.2.cloned.1.call-start = ((), (), s32[]{:S(2)}) async-start(), calls=%async_computation | async-start | bytes 1769472 | tf_op jit(solution)/shard_map/all_gather | solution.py:82
  38.9 7.3 %copy-start.1 = (bf16[768,4,2,128]{3,0,1,2:T(8,128)(2,1)S(1)}, bf16[768,4,2,128]{3,0,1,2:T(8,128)(2,1)}, u32[]{:S(2)}) copy-start(bf16[768,4,2,128]{3,0,1,2:T(8,128)(2,1)} %all-gather.2.cloned.1.call-done) | copy-start | bytes 4718596
  52.5 25.4 %collective-permute-start = (bf16[1,64,64,128]{3,2,1,0:T(8,128)(2,1)S(1)}, bf16[1,64,64,128]{3,2,1,0:T(8,128)(2,1)S(1)}, u32[]{:S(2)}, u32[]{:S(2)}) collective-permute-start(bf16[1,64,64,128]{3,2,1,0:T(8,128)(2,1)S(1)} %copy.21), channel_id=1, source_target_pairs={{0,16},{16,0},{1,17},{17,1},{2,18},{18,2},{3,19},{19,3},{4,20},{20... | collective-permute-start | bytes 3145736 | tf_op jit(solution)/shard_map/ppermute | solution.py:12
Sparse Core Ops, SparseCore 0:
  11.1 27.7 all-gather.1
where the time goes:
time: 86 us; the launch traced here: 85.7 us
  waiting for transfers between devices  50 us (58%)
  between operations  13.5 us (16%)
  matrix products  9.58 us (11%)
  other arithmetic  7.25 us (8%)
  local copies, waits for them, and re-layouts  3.72 us (4%)
  starting transfers between devices  1.54 us (2%)
    all_gather x1, waiting for transfers between devices, on_device(): lax.all_gather(own_block, 'ctx', axis=0, tiled=True)  26.2 us
    ppermute x1, waiting for transfers between devices, shifted(): return lax.ppermute(value, axis, pairs)  23.8 us
    dot_general x1, matrix products, attend(): jnp.einsum('tgqd,kgd->gqtk', grouped, keys, preferred_element_type=jnp.fl...  4 us
    reduce_sum x1, other arithmetic, attend(): total = total * rescale + jnp.sum(expo, axis=-1)  3.29 us
    dot_general x1, matrix products, attend(): jnp.einsum('gqtk,kgd->gqtd', expo.astype(jnp.bfloat16), vals, preferred_e...  3.1 us
    unnamed x7, local copies, waits for them, and re-layouts  2.77 us
    dot_general x1, matrix products, on_device(): jnp.dot(mixed.reshape(-1, width), hadamard(width), precision=lax.Precisio...  2.48 us
  transfers between devices with their start and end apart: 2, of which 2 were waited for; matrix products, arithmetic and copies ran while one was open for 2% of the time, Pallas kernels for 0%

commit v1 on v0

v1 whole, which is shorter than its diff:
```python
import functools
import math

import jax
import jax.numpy as jnp
from jax import lax
from jax.experimental import pallas as pl
from jax.experimental.pallas import tpu as pltpu
from jax.sharding import PartitionSpec as P

CBLK = 16
LANES = 128
HIDDEN = -1e30
TILE_TOKENS = 16


def hadamard_signs(order):
    rows = lax.broadcasted_iota(jnp.int32, (order, order), 0)
    both = rows & lax.broadcasted_iota(jnp.int32, (order, order), 1)
    common = jnp.zeros((order, order), jnp.int32)
    for bit in range(order.bit_length() - 1):
        common = common + (jnp.right_shift(both, bit) & 1)
    return (1 - 2 * (common & 1)).astype(jnp.float32).astype(jnp.bfloat16)


def power_of_two(exponent):
    value = jnp.float32(2.0)
    for candidate in range(-3, 1):
        value = jnp.where(exponent == candidate, jnp.float32(2.0**candidate), value)
    return value


def kernel(
    sections, owners, q_ref, sk_ref, sv_ref, ck_ref, cv_ref, exps_ref, order_ref, out_ref,
    raw_span, raw_ctx, wide, stage, kv_far, kv_near, q_far, q_near, mixed, order_near, order_far, bias,
    load_sem, near_sem, ring_send, ring_recv, pair_send, pair_recv, query_send, query_recv,
    result_send, result_recv, store_sem,
):
    pipe, mine = lax.axis_index("pipe"), lax.axis_index("ctx")
    onward = lax.rem(pipe + 1, sections)
    before = lax.rem(pipe + sections - 1, sections)
    chips = owners // 2
    chip, core = lax.div(mine, 2), lax.rem(mine, 2)
    twin = chip * 2 + 1 - core
    tokens = q_ref.shape[1]
    kv_local = sk_ref.shape[2]
    group = q_ref.shape[2] // kv_local
    width = q_ref.shape[3]
    cache_len = ck_ref.shape[1]
    rows_dev = cache_len + tokens
    half = tokens // 2
    far_heads = kv_far.shape[0]
    near_heads = kv_near.shape[0]
    slot = pl.ds(pl.multiple_of(mine * rows_dev, 16), rows_dev)

    loads = [
        pltpu.make_async_copy(sk_ref.at[0], raw_span.at[0], load_sem.at[0]),
        pltpu.make_async_copy(sv_ref.at[0], raw_span.at[1], load_sem.at[1]),
        pltpu.make_async_copy(ck_ref.at[0], raw_ctx.at[0], load_sem.at[2]),
        pltpu.make_async_copy(cv_ref.at[0], raw_ctx.at[1], load_sem.at[3]),
    ]
    for load in loads:
        load.start()

    def heads(kv_head):
        return pl.ds(kv_head * group, group)

    barrier = pltpu.get_barrier_semaphore()
    pl.semaphore_signal(barrier, inc=1, device_id={"pipe": onward})
    greeted = 2
    if sections > 2:
        pl.semaphore_signal(barrier, inc=1, device_id={"pipe": before})
        greeted = 3
    pl.semaphore_signal(barrier, inc=1, device_id={"ctx": twin})

    @pl.when(chip > 0)
    def _():
        pl.semaphore_signal(barrier, inc=1, device_id={"ctx": mine - 2})

    @pl.when(chip < chips - 1)
    def _():
        pl.semaphore_signal(barrier, inc=1, device_id={"ctx": mine + 2})

    signs = hadamard_signs(width)
    for block in range(2 * owners):
        order_near[block : block + 1, :] = jnp.full((1, LANES), order_ref[0, block], jnp.int32)

    for neighbour in (chip > 0, chip < chips - 1):
        greeted = greeted + neighbour.astype(jnp.int32)
    pl.semaphore_wait(barrier, greeted)

    query_sends = [
        pltpu.make_async_remote_copy(
            q_ref.at[0, :, heads(head), :], q_far.at[head], query_send.at[head], query_recv.at[head],
            device_id={"pipe": onward},
        )
        for head in range(far_heads)
    ]
    query_sends[0].start()
    near_loads = [
        pltpu.make_async_copy(q_ref.at[0, :, heads(far_heads + head), :], q_near.at[head], near_sem.at[head])
        for head in range(near_heads)
    ]

    for load in loads:
        load.wait()
    for kind in range(2):
        wide[kind, :cache_len] = raw_ctx[kind].astype(jnp.float32)
        wide[kind, cache_len:] = raw_span[kind].astype(jnp.float32)

    def prepared(kv_head, kind):
        rows = wide[kind, :, kv_head, :]
        parts = [
            rows[block * CBLK : (block + 1) * CBLK] * power_of_two(exps_ref[0, block, kv_head, kind])
            for block in range(cache_len // CBLK)
        ]
        rows = jnp.concatenate(parts + [rows[cache_len:]], axis=0).astype(jnp.bfloat16)
        if kind == 1:
            rows = jnp.dot(rows, signs, preferred_element_type=jnp.float32).astype(jnp.bfloat16)
        return rows

    def block_copy(which, way, owner, target):
        held = (kv_far, kv_near)[which]
        part = held.at[:, :, pl.ds(pl.multiple_of(owner * rows_dev, 16), rows_dev), :]
        return pltpu.make_async_remote_copy(
            part, part, ring_send.at[which, way, owner], ring_recv.at[which, owner], device_id={"ctx": target}
        )

    def move(which, owner, way, act):
        target = (mine + 2, mine - 2, twin)[way]
        if way == 2:
            act(block_copy(which, way, owner, target))
        else:

            @pl.when((chip < chips - 1) if way == 0 else (chip > 0))
            def _():
                act(block_copy(which, way, owner, target))

    def send(copy):
        copy.start()

    def sent(copy):
        copy.wait_send()

    def own_block(which, act):
        for way in range(3):
            move(which, mine, way, act)

    def step(which, distance, act, waiting):
        for way, there, owner in (
            (0, chip >= distance, mine - 2 * distance),
            (1, chip + distance < chips, mine + 2 * distance),
        ):

            @pl.when(there)
            def _():
                if waiting:
                    block_copy(which, 2, owner, twin).wait_recv()
                move(which, owner, way, act)
                move(which, owner, 2, act)

    def twin_blocks(which):
        for other in range(chips):
            block_copy(which, 2, 2 * other + 1 - core, twin).wait_recv()

    for head in range(near_heads):
        for kind in range(2):
            kv_near[head, kind, slot, :] = prepared(far_heads + head, kind)
    own_block(1, send)
    for load in near_loads:
        load.start()
    for head in range(far_heads):
        for kind in range(2):
            stage[head, kind] = prepared(head, kind)
    pair_sends = [
        pltpu.make_async_remote_copy(
            stage, kv_far.at[:, :, slot, :], pair_send.at[0], pair_recv.at[0], device_id={"pipe": onward}
        ),
        pltpu.make_async_remote_copy(
            order_near, order_far, pair_send.at[1], pair_recv.at[1], device_id={"pipe": onward}
        ),
    ]
    for copy in pair_sends:
        copy.start()
    for copy in query_sends[1:]:
        copy.start()

    def fill_bias(order):
        token = lax.div(lax.broadcasted_iota(jnp.int32, (tokens * group, LANES), 0), group)
        first = order[pl.ds(2 * mine, 1), :]
        second = order[pl.ds(2 * mine + 1, 1), :]
        place = jnp.where(token < half, first, second) * half + lax.rem(token, half)
        for tile in range(owners * rows_dev // LANES):
            column = tile * LANES + lax.broadcasted_iota(jnp.int32, (1, LANES), 1)
            key_place = jnp.full((1, LANES), -1, jnp.int32)
            for block in range(2 * owners):
                start = (block // 2) * rows_dev + cache_len + (block % 2) * half
                if start < (tile + 1) * LANES and start + half > tile * LANES:
                    inside = (column >= start) & (column < start + half)
                    key_place = jnp.where(inside, order[block : block + 1, :] * half + column - start, key_place)
            bias[:, tile * LANES : (tile + 1) * LANES] = jnp.where(key_place <= place, 0.0, HIDDEN)

    scale = math.log2(math.e) / width**0.5
    shrink = 1.0 / width**0.5
    rows_tile = TILE_TOKENS * group

    def attend(queries, held, head, target):
        @pl.loop(0, tokens // TILE_TOKENS)
        def _(tile):
            part = pl.ds(pl.multiple_of(tile * TILE_TOKENS, TILE_TOKENS), TILE_TOKENS)
            rows = pl.ds(pl.multiple_of(tile * rows_tile, rows_tile), rows_tile)
            query = queries[head, part].reshape(rows_tile, width)
            score = lax.dot_general(
                query, held[head, 0], (((1,), (1,)), ((), ())), preferred_element_type=jnp.float32
            )
            score = score * scale + bias[rows, :]
            top = jnp.max(score, axis=-1, keepdims=True)
            weight = jnp.exp2(score - top).astype(jnp.bfloat16)
            values = held[head, 1]
            both = jnp.concatenate([values, jnp.ones_like(values)], axis=1)
            total = jnp.dot(weight, both, preferred_element_type=jnp.float32)
            result = total[:, :width] * (shrink / total[:, width:])
            mixed[target, part] = result.astype(jnp.bfloat16).reshape(TILE_TOKENS, group, width)

    fill_bias(order_near)
    step(1, 1, send, True)
    pair_sends[0].wait_recv()
    own_block(0, send)
    for distance in range(2, chips):
        step(1, distance, send, True)
    twin_blocks(1)
    pending = list(range(1, chips))
    result_sends = []
    for head in range(near_heads):
        if pending:
            step(0, pending.pop(0), send, True)
        near_loads[head].wait()
        attend(q_near, kv_near, head, far_heads + head)
        copy = pltpu.make_async_remote_copy(
            mixed.at[far_heads + head], out_ref.at[0, :, heads(far_heads + head), :],
            result_send.at[head], result_recv.at[head], device_id={"pipe": onward},
        )
        copy.start()
        result_sends.append(copy)
    for distance in pending:
        step(0, distance, send, True)
    pair_sends[1].wait_recv()
    fill_bias(order_far)
    twin_blocks(0)
    stores = []
    for head in range(far_heads):
        query_sends[head].wait_recv()
        attend(q_far, kv_far, head, head)
        copy = pltpu.make_async_copy(mixed.at[head], out_ref.at[0, :, heads(head), :], store_sem.at[head])
        copy.start()
        stores.append(copy)

    for which in range(2):
        own_block(which, sent)
        for distance in range(1, chips):
            step(which, distance, sent, False)
    for copy in pair_sends + query_sends:
        copy.wait_send()
    for copy in stores:
        copy.wait()
    for copy in result_sends:
        copy.wait()


def on_device(queries, span_keys, span_values, cache_keys, cache_values, scale_exps, block_order):
    sections, owners = lax.axis_size("pipe"), lax.axis_size("ctx")
    tokens, head_local, width = queries.shape[1:]
    kv_local = span_keys.shape[2]
    group = head_local // kv_local
    cache_len = cache_keys.shape[1]
    rows_dev = cache_len + tokens
    far, near = kv_local // 2, kv_local - kv_local // 2
    anywhere = pl.BlockSpec(memory_space=pl.ANY)
    scalars = pl.BlockSpec(memory_space=pltpu.SMEM)
    dma = pltpu.SemaphoreType.DMA
    return pl.pallas_call(
        functools.partial(kernel, sections, owners),
        out_shape=jax.ShapeDtypeStruct(queries.shape, jnp.bfloat16),
        in_specs=[anywhere] * 5 + [scalars] * 2,
        out_specs=anywhere,
        scratch_shapes=[
            pltpu.VMEM((2, tokens, kv_local, width), jnp.bfloat16),
            pltpu.VMEM((2, cache_len, kv_local, width), jnp.bfloat16),
            pltpu.VMEM((2, rows_dev, kv_local, width), jnp.float32),
            pltpu.VMEM((far, 2, rows_dev, width), jnp.bfloat16),
            pltpu.VMEM((far, 2, owners * rows_dev, width), jnp.bfloat16),
            pltpu.VMEM((near, 2, owners * rows_dev, width), jnp.bfloat16),
            pltpu.VMEM((far, tokens, group, width), jnp.bfloat16),
            pltpu.VMEM((near, tokens, group, width), jnp.bfloat16),
            pltpu.VMEM((kv_local, tokens, group, width), jnp.bfloat16),
            pltpu.VMEM((2 * owners, LANES), jnp.int32),
            pltpu.VMEM((2 * owners, LANES), jnp.int32),
            pltpu.VMEM((tokens * group, owners * rows_dev), jnp.float32),
            dma((4,)),
            dma((near,)),
            dma((2, 3, owners)),
            dma((2, owners)),
            dma((2,)),
            dma((2,)),
            dma((far,)),
            dma((far,)),
            dma((near,)),
            dma((near,)),
            dma((far,)),
        ],
        compiler_params=pltpu.CompilerParams(
            collective_id=0, has_side_effects=True, vmem_limit_bytes=48 * 1024 * 1024
        ),
    )(queries, span_keys, span_values, cache_keys, cache_values, scale_exps, block_order)


def solution(mesh):
    placed = P("pipe", "ctx", "tp", None)
    return jax.shard_map(
        on_device,
        mesh=mesh,
        in_specs=(placed,) * 6 + (P("pipe", None),),
        out_specs=placed,
        check_vma=False,
    )
```

time: 86 us -> 44 us (0.51)
  waiting for transfers between devices: 50 us -> 0 us
  Pallas kernels: 0 us -> 37.4 us
  between operations: 13.5 us -> 0.02 us
  matrix products: 9.58 us -> 0 us
  other arithmetic: 7.25 us -> 0 us
  local copies, waits for them, and re-layouts: 3.72 us -> 6.18 us
  starting transfers between devices: 1.54 us -> 0 us
    pallas_call x0 -> x1, Pallas kernels: none -> 37.4 us  [on_device(): pl.pallas_call(functools.partial(kernel, sections, owners), out_shape=jax...]
    all_gather x1 -> x0, waiting for transfers between devices: 26.2 us -> none  [on_device(): lax.all_gather(own_block, 'ctx', axis=0, tiled=True)]
    ppermute x1 -> x0, waiting for transfers between devices: 23.8 us -> none  [shifted(): return lax.ppermute(value, axis, pairs)]
    dot_general x3 -> x0, matrix products: 9.58 us -> none  [the longest x1 4 us: attend(): jnp.einsum('tgqd,kgd->gqtk', grouped, keys, preferred_element_type=jnp.fl...]
    reduce_sum x3 -> x0, other arithmetic: 4.78 us -> none  [the longest x1 3.29 us: attend(): total = total * rescale + jnp.sum(expo, axis=-1)]
    unnamed x7 -> x14, local copies, waits for them, and re-layouts: 2.77 us -> 6.18 us
    ppermute x1 -> x0, starting transfers between devices: 1.53 us -> none  [shifted(): return lax.ppermute(value, axis, pairs)]
    convert_element_type x1 -> x0, other arithmetic: 0.87 us -> none  [on_device(): (cache_values[0].astype(jnp.float32) * factor[:, :, 1:2]).astype(jnp.bflo...]
  transfers between devices with their start and end apart: 2 -> 0, of which waited for: 2 -> 0; matrix products, arithmetic and copies ran while one was open for 2% -> 0% of each run, Pallas kernels for 0% -> 0%
where the time goes in v1:
time: 44 us; the launch traced here: 43.6 us
  Pallas kernels  37.4 us (85%)
  local copies, waits for them, and re-layouts  6.18 us (14%)
    pallas_call x1, Pallas kernels, on_device(): pl.pallas_call(functools.partial(kernel, sections, owners), out_shape=jax...  37.4 us
    unnamed x14, local copies, waits for them, and re-layouts  6.18 us

profile of v1, /device:TPU:0, one launch (start us, length us, event | category | flops | bytes accessed | tf_op | source)
XLA Modules:
  0.0 43.6 jit_solution(12541737682667938612)
XLA Ops:
  0.0 0.0 copy-start.5
  0.0 0.8 %copy.8.exps_ref = s32[1,2,4,2]{3,2,1,0:T(4,128)S(1)} copy(s32[1,2,4,2]{2,3,1,0:T(2,128)} %param.12) | data formatting | bytes 128 | tf_op args[5]
  0.8 0.0 copy-done.5
  0.8 0.0 copy-start
  0.8 1.2 %copy-done = bf16[1,64,64,128]{3,2,1,0:T(8,128)(2,1)S(1)} copy-done((bf16[1,64,64,128]{3,2,1,0:T(8,128)(2,1)S(1)}, bf16[1,64,64,128]{3,2,1,0:T(8,128)(2,1)}, u32[]{:S(2)}) %copy-start) | copy-done | bytes 1048600
  2.0 0.0 copy-start.1
  2.0 0.8 %copy-done.1 = bf16[1,64,4,128]{3,2,1,0:T(4,128)(2,1)S(1)} copy-done((bf16[1,64,4,128]{3,2,1,0:T(4,128)(2,1)S(1)}, bf16[1,64,4,128]{3,2,1,0:T(4,128)(2,1)}, u32[]{:S(2)}) %copy-start.1) | copy-done | bytes 65560
  2.9 0.0 copy-start.2
  2.9 0.8 %copy-done.2 = bf16[1,64,4,128]{3,2,1,0:T(4,128)(2,1)S(1)} copy-done((bf16[1,64,4,128]{3,2,1,0:T(4,128)(2,1)S(1)}, bf16[1,64,4,128]{3,2,1,0:T(4,128)(2,1)}, u32[]{:S(2)}) %copy-start.2) | copy-done | bytes 65560
  3.7 0.0 copy-start.3
  3.7 0.8 %copy-done.3 = bf16[1,32,4,128]{3,2,1,0:T(4,128)(2,1)S(1)} copy-done((bf16[1,32,4,128]{3,2,1,0:T(4,128)(2,1)S(1)}, bf16[1,32,4,128]{3,2,1,0:T(4,128)(2,1)}, u32[]{:S(2)}) %copy-start.3) | copy-done | bytes 32792
  4.5 0.0 copy-start.4
  4.5 0.8 %copy-done.4 = bf16[1,32,4,128]{3,2,1,0:T(4,128)(2,1)S(1)} copy-done((bf16[1,32,4,128]{3,2,1,0:T(4,128)(2,1)S(1)}, bf16[1,32,4,128]{3,2,1,0:T(4,128)(2,1)}, u32[]{:S(2)}) %copy-start.4) | copy-done | bytes 32792
  5.2 37.4 %shard_map.73 = bf16[1,64,64,128]{3,2,1,0:T(8,128)(2,1)S(1)} custom-call(bf16[1,64,64,128]{3,2,1,0:T(8,128)(2,1)S(1)} %copy-done, bf16[1,64,4,128]{3,2,1,0:T(4,128)(2,1)S(1)} %copy-done.1, bf16[1,64,4,128]{3,2,1,0:T(4,128)(2,1)S(1)} %copy-done.2, bf16[1,32,4,128]{3,2,1,0:T(4,128)(2,1)S(1)} %copy-done.3, bf16[1,32,4,128]{3,2,1,0:T(4,128)(2,1)S(1)} %copy-done.4, ...), custom_call_target="tpu_custom_call" | custom-call | tf_op jit(solution)/shard_map/pallas_call | solution.py:281
  42.6 1.0 %copy.10 = bf16[1,64,64,128]{3,2,1,0:T(8,128)(2,1)} copy(bf16[1,64,64,128]{3,2,1,0:T(8,128)(2,1)S(1)} %shard_map.73) | data formatting | bytes 2097152
Async XLA Ops:
  0.0 0.8 %copy-start.5 = (s32[1,16]{1,0:T(1,128)S(1)}, s32[1,16]{1,0:T(1,128)}, u32[]{:S(2)}) copy-start(s32[1,16]{1,0:T(1,128)} %order_ref.1) | copy-start | bytes 196
  0.8 1.2 %copy-start = (bf16[1,64,64,128]{3,2,1,0:T(8,128)(2,1)S(1)}, bf16[1,64,64,128]{3,2,1,0:T(8,128)(2,1)}, u32[]{:S(2)}) copy-start(bf16[1,64,64,128]{3,2,1,0:T(8,128)(2,1)} %q_ref.1) | copy-start | bytes 3145732
  2.0 0.8 %copy-start.1 = (bf16[1,64,4,128]{3,2,1,0:T(4,128)(2,1)S(1)}, bf16[1,64,4,128]{3,2,1,0:T(4,128)(2,1)}, u32[]{:S(2)}) copy-start(bf16[1,64,4,128]{3,2,1,0:T(4,128)(2,1)} %sk_ref.1) | copy-start | bytes 196612
  2.9 0.8 %copy-start.2 = (bf16[1,64,4,128]{3,2,1,0:T(4,128)(2,1)S(1)}, bf16[1,64,4,128]{3,2,1,0:T(4,128)(2,1)}, u32[]{:S(2)}) copy-start(bf16[1,64,4,128]{3,2,1,0:T(4,128)(2,1)} %sv_ref.1) | copy-start | bytes 196612
  3.7 0.8 %copy-start.3 = (bf16[1,32,4,128]{3,2,1,0:T(4,128)(2,1)S(1)}, bf16[1,32,4,128]{3,2,1,0:T(4,128)(2,1)}, u32[]{:S(2)}) copy-start(bf16[1,32,4,128]{3,2,1,0:T(4,128)(2,1)} %ck_ref.1) | copy-start | bytes 98308
  4.5 0.8 %copy-start.4 = (bf16[1,32,4,128]{3,2,1,0:T(4,128)(2,1)S(1)}, bf16[1,32,4,128]{3,2,1,0:T(4,128)(2,1)}, u32[]{:S(2)}) copy-start(bf16[1,32,4,128]{3,2,1,0:T(4,128)(2,1)} %cv_ref.1) | copy-start | bytes 98308

commit v2 on v1

--- a/solution.py
+++ b/solution.py
@@ -12,6 +12,7 @@
 LANES = 128
 HIDDEN = -1e30
 TILE_TOKENS = 16
+REACH = 2
 
 
 def hadamard_signs(order):
@@ -33,7 +34,7 @@
 def kernel(
     sections, owners, q_ref, sk_ref, sv_ref, ck_ref, cv_ref, exps_ref, order_ref, out_ref,
     raw_span, raw_ctx, wide, stage, kv_far, kv_near, q_far, q_near, mixed, order_near, order_far, bias,
-    load_sem, near_sem, ring_send, ring_recv, pair_send, pair_recv, query_send, query_recv,
+    load_sem, near_sem, far_send, far_recv, near_send, near_recv, pair_send, pair_recv, query_send, query_recv,
     result_send, result_recv, store_sem,
 ):
     pipe, mine = lax.axis_index("pipe"), lax.axis_index("ctx")
@@ -71,22 +72,22 @@
     if sections > 2:
         pl.semaphore_signal(barrier, inc=1, device_id={"pipe": before})
         greeted = 3
+    for distance in range(1, min(REACH, chips - 1) + 1):
+        for near_enough in (chip >= distance, chip + distance < chips):
+            greeted = greeted + near_enough.astype(jnp.int32)
     pl.semaphore_signal(barrier, inc=1, device_id={"ctx": twin})
 
-    @pl.when(chip > 0)
-    def _():
-        pl.semaphore_signal(barrier, inc=1, device_id={"ctx": mine - 2})
-
-    @pl.when(chip < chips - 1)
-    def _():
-        pl.semaphore_signal(barrier, inc=1, device_id={"ctx": mine + 2})
+    for distance in range(1, min(REACH, chips - 1) + 1):
+        for there, other in ((chip >= distance, mine - 2 * distance), (chip + distance < chips, mine + 2 * distance)):
+
+            @pl.when(there)
+            def _():
+                pl.semaphore_signal(barrier, inc=1, device_id={"ctx": other})
 
     signs = hadamard_signs(width)
     for block in range(2 * owners):
         order_near[block : block + 1, :] = jnp.full((1, LANES), order_ref[0, block], jnp.int32)
 
-    for neighbour in (chip > 0, chip < chips - 1):
-        greeted = greeted + neighbour.astype(jnp.int32)
     pl.semaphore_wait(barrier, greeted)
 
     query_sends = [
@@ -96,7 +97,6 @@
         )
         for head in range(far_heads)
     ]
-    query_sends[0].start()
     near_loads = [
         pltpu.make_async_copy(q_ref.at[0, :, heads(far_heads + head), :], q_near.at[head], near_sem.at[head])
         for head in range(near_heads)
@@ -111,7 +111,7 @@
     def prepared(kv_head, kind):
         rows = wide[kind, :, kv_head, :]
         parts = [
-            rows[block * CBLK : (block + 1) * CBLK] * power_of_two(exps_ref[0, block, kv_head, kind])
+            rows[block * CBLK : (block + 1) * CBLK] * power_of_two(exps_ref[0, block, kind, kv_head])
             for block in range(cache_len // CBLK)
         ]
         rows = jnp.concatenate(parts + [rows[cache_len:]], axis=0).astype(jnp.bfloat16)
@@ -119,22 +119,22 @@
             rows = jnp.dot(rows, signs, preferred_element_type=jnp.float32).astype(jnp.bfloat16)
         return rows
 
-    def block_copy(which, way, owner, target):
+    def block_copy(which, head, way, owner, target):
         held = (kv_far, kv_near)[which]
-        part = held.at[:, :, pl.ds(pl.multiple_of(owner * rows_dev, 16), rows_dev), :]
+        part = held.at[head, :, pl.ds(pl.multiple_of(owner * rows_dev, 16), rows_dev), :]
         return pltpu.make_async_remote_copy(
-            part, part, ring_send.at[which, way, owner], ring_recv.at[which, owner], device_id={"ctx": target}
+            part,
+            part,
+            (far_send, near_send)[which].at[head, way],
+            (far_recv, near_recv)[which].at[head, owner],
+            device_id={"ctx": target},
         )
 
-    def move(which, owner, way, act):
-        target = (mine + 2, mine - 2, twin)[way]
-        if way == 2:
-            act(block_copy(which, way, owner, target))
-        else:
-
-            @pl.when((chip < chips - 1) if way == 0 else (chip > 0))
-            def _():
-                act(block_copy(which, way, owner, target))
+    def others(distance):
+        return (
+            (chip + distance < chips, mine + 2 * distance, distance),
+            (chip >= distance, mine - 2 * distance, chips + distance),
+        )
 
     def send(copy):
         copy.start()
@@ -142,31 +142,49 @@
     def sent(copy):
         copy.wait_send()
 
+    def own_head(which, head, act):
+        for distance in range(min(REACH, chips - 1), 0, -1):
+            for there, other, way in others(distance):
+
+                @pl.when(there)
+                def _():
+                    act(block_copy(which, head, way, mine, other))
+
+        act(block_copy(which, head, 0, mine, twin))
+
     def own_block(which, act):
-        for way in range(3):
-            move(which, mine, way, act)
+        for head in range((far_heads, near_heads)[which]):
+            own_head(which, head, act)
 
     def step(which, distance, act, waiting):
-        for way, there, owner in (
-            (0, chip >= distance, mine - 2 * distance),
-            (1, chip + distance < chips, mine + 2 * distance),
-        ):
-
-            @pl.when(there)
-            def _():
-                if waiting:
-                    block_copy(which, 2, owner, twin).wait_recv()
-                move(which, owner, way, act)
-                move(which, owner, 2, act)
+        ahead = ((chip > 0, mine - 2), (chip < chips - 1, mine + 2))
+        for (there, other, way), (further, following) in zip(others(distance), ahead):
+            for head in range((far_heads, near_heads)[which]):
+
+                @pl.when(there)
+                def _():
+                    if waiting:
+                        block_copy(which, head, 0, other, twin).wait_recv()
+
+                if distance >= REACH:
+
+                    @pl.when(there & further)
+                    def _():
+                        act(block_copy(which, head, 4 * chips + way, other, following))
+
+                @pl.when(there)
+                def _():
+                    act(block_copy(which, head, 2 * chips + way, other, twin))
 
     def twin_blocks(which):
         for other in range(chips):
-            block_copy(which, 2, 2 * other + 1 - core, twin).wait_recv()
+            for head in range((far_heads, near_heads)[which]):
+                block_copy(which, head, 0, 2 * other + 1 - core, twin).wait_recv()
 
     for head in range(near_heads):
         for kind in range(2):
             kv_near[head, kind, slot, :] = prepared(far_heads + head, kind)
-    own_block(1, send)
+        own_head(1, head, send)
     for load in near_loads:
         load.start()
     for head in range(far_heads):
@@ -182,7 +200,7 @@
     ]
     for copy in pair_sends:
         copy.start()
-    for copy in query_sends[1:]:
+    for copy in query_sends:
         copy.start()
 
     def fill_bias(order):
@@ -204,7 +222,7 @@
     shrink = 1.0 / width**0.5
     rows_tile = TILE_TOKENS * group
 
-    def attend(queries, held, head, target):
+    def attend(queries, held, head, target, done=None):
         @pl.loop(0, tokens // TILE_TOKENS)
         def _(tile):
             part = pl.ds(pl.multiple_of(tile * TILE_TOKENS, TILE_TOKENS), TILE_TOKENS)
@@ -221,27 +239,31 @@
             total = jnp.dot(weight, both, preferred_element_type=jnp.float32)
             result = total[:, :width] * (shrink / total[:, width:])
             mixed[target, part] = result.astype(jnp.bfloat16).reshape(TILE_TOKENS, group, width)
+            if done is not None:
+                done(tile)
 
     fill_bias(order_near)
-    step(1, 1, send, True)
+    if chips > REACH:
+        step(1, REACH, send, True)
     pair_sends[0].wait_recv()
     own_block(0, send)
-    for distance in range(2, chips):
+    for distance in list(range(1, min(REACH, chips))) + list(range(REACH + 1, chips)):
         step(1, distance, send, True)
     twin_blocks(1)
-    pending = list(range(1, chips))
-    result_sends = []
+    pending = [distance for distance in range(REACH, chips)] + list(range(1, min(REACH, chips)))
+
+    def result_copy(head, tile):
+        part = pl.ds(pl.multiple_of(tile * TILE_TOKENS, TILE_TOKENS), TILE_TOKENS)
+        return pltpu.make_async_remote_copy(
+            mixed.at[far_heads + head, part], out_ref.at[0, part, heads(far_heads + head), :],
+            result_send.at[head, tile], result_recv.at[head, tile], device_id={"pipe": onward},
+        )
+
     for head in range(near_heads):
+        near_loads[head].wait()
+        attend(q_near, kv_near, head, far_heads + head, lambda tile: result_copy(head, tile).start())
         if pending:
             step(0, pending.pop(0), send, True)
-        near_loads[head].wait()
-        attend(q_near, kv_near, head, far_heads + head)
-        copy = pltpu.make_async_remote_copy(
-            mixed.at[far_heads + head], out_ref.at[0, :, heads(far_heads + head), :],
-            result_send.at[head], result_recv.at[head], device_id={"pipe": onward},
-        )
-        copy.start()
-        result_sends.append(copy)
     for distance in pending:
         step(0, distance, send, True)
     pair_sends[1].wait_recv()
@@ -263,8 +285,9 @@
         copy.wait_send()
     for copy in stores:
         copy.wait()
-    for copy in result_sends:
-        copy.wait()
+    for head in range(near_heads):
+        for tile in range(tokens // TILE_TOKENS):
+            result_copy(head, tile).wait()
 
 
 def on_device(queries, span_keys, span_values, cache_keys, cache_values, scale_exps, block_order):
@@ -298,20 +321,22 @@
             pltpu.VMEM((tokens * group, owners * rows_dev), jnp.float32),
             dma((4,)),
             dma((near,)),
-            dma((2, 3, owners)),
-            dma((2, owners)),
+            dma((far, 3 * owners)),
+            dma((far, owners)),
+            dma((near, 3 * owners)),
+            dma((near, owners)),
             dma((2,)),
             dma((2,)),
             dma((far,)),
             dma((far,)),
-            dma((near,)),
-            dma((near,)),
+            dma((near, tokens // TILE_TOKENS)),
+            dma((near, tokens // TILE_TOKENS)),
             dma((far,)),
         ],
         compiler_params=pltpu.CompilerParams(
-            collective_id=0, has_side_effects=True, vmem_limit_bytes=48 * 1024 * 1024
+            collective_id=0, has_side_effects=True, vmem_limit_bytes=62 * 1024 * 1024
         ),
-    )(queries, span_keys, span_values, cache_keys, cache_values, scale_exps, block_order)
+    )(queries, span_keys, span_values, cache_keys, cache_values, scale_exps.swapaxes(2, 3), block_order)
 
 
 def solution(mesh):

time: 44 us -> 36.1 us (0.82)
  local copies, waits for them, and re-layouts: 6.18 us -> 2.26 us
  Pallas kernels: 37.4 us -> 33.6 us
    unnamed x14 -> x1, local copies, waits for them, and re-layouts: 6.18 us -> 2.26 us
    pallas_call x1, Pallas kernels: 37.4 us -> 33.6 us  [on_device(): pl.pallas_call(functools.partial(kernel, sections, owners), out_shape=jax...]
where the time goes in v2:
time: 36.1 us; the launch traced here: 35.9 us
  Pallas kernels  33.6 us (93%)
  local copies, waits for them, and re-layouts  2.26 us (6%)
    pallas_call x1, Pallas kernels, on_device(): pl.pallas_call(functools.partial(kernel, sections, owners), out_shape=jax...  33.6 us
    unnamed x1, local copies, waits for them, and re-layouts  2.26 us

profile of v2, /device:TPU:0, one launch (start us, length us, event | category | flops | bytes accessed | tf_op | source)
XLA Modules:
  0.0 35.9 jit_solution(5679027390742366735)
XLA Ops:
  0.0 33.6 %shard_map.73 = bf16[1,64,64,128]{3,2,1,0:T(8,128)(2,1)} custom-call(bf16[1,64,64,128]{3,2,1,0:T(8,128)(2,1)} %q_ref.1, bf16[1,64,4,128]{3,2,1,0:T(4,128)(2,1)} %sk_ref.1, bf16[1,64,4,128]{3,2,1,0:T(4,128)(2,1)} %sv_ref.1, bf16[1,32,4,128]{3,2,1,0:T(4,128)(2,1)} %ck_ref.1, bf16[1,32,4,128]{3,2,1,0:T(4,128)(2,1)} %cv_ref.1, s32[1,2,2,4]{3,2,1,0:T(2,128)} %bitcast.1, ...), custom_call_target="tpu_custom_call" | custom-call | tf_op jit(solution)/shard_map/pallas_call | solution.py:304
  33.6 2.3 %copy.9 = bf16[1,64,64,128]{3,2,1,0:T(8,128)(2,1)} copy(bf16[1,64,64,128]{3,2,1,0:T(8,128)(2,1)} %shard_map.73) | data formatting | bytes 2097152

commit v3 on v2

--- a/solution.py
+++ b/solution.py
@@ -88,7 +88,6 @@
     for block in range(2 * owners):
         order_near[block : block + 1, :] = jnp.full((1, LANES), order_ref[0, block], jnp.int32)
 
-    pl.semaphore_wait(barrier, greeted)
 
     query_sends = [
         pltpu.make_async_remote_copy(
@@ -181,15 +180,13 @@
             for head in range((far_heads, near_heads)[which]):
                 block_copy(which, head, 0, 2 * other + 1 - core, twin).wait_recv()
 
+    for head in range(far_heads):
+        for kind in range(2):
+            stage[head, kind] = prepared(head, kind)
     for head in range(near_heads):
         for kind in range(2):
             kv_near[head, kind, slot, :] = prepared(far_heads + head, kind)
-        own_head(1, head, send)
-    for load in near_loads:
-        load.start()
-    for head in range(far_heads):
-        for kind in range(2):
-            stage[head, kind] = prepared(head, kind)
+    pl.semaphore_wait(barrier, greeted)
     pair_sends = [
         pltpu.make_async_remote_copy(
             stage, kv_far.at[:, :, slot, :], pair_send.at[0], pair_recv.at[0], device_id={"pipe": onward}
@@ -202,6 +199,9 @@
         copy.start()
     for copy in query_sends:
         copy.start()
+    own_block(1, send)
+    for load in near_loads:
+        load.start()
 
     def fill_bias(order):
         token = lax.div(lax.broadcasted_iota(jnp.int32, (tokens * group, LANES), 0), group)

time: 36.1 us -> 35.5 us (0.983)
  Pallas kernels: 33.6 us -> 33 us
    pallas_call x1, Pallas kernels: 33.6 us -> 33 us  [on_device(): pl.pallas_call(functools.partial(kernel, sections, owners), out_shape=jax...]
where the time goes in v3:
time: 35.5 us; the launch traced here: 35.3 us
  Pallas kernels  33 us (93%)
  local copies, waits for them, and re-layouts  2.26 us (6%)
    pallas_call x1, Pallas kernels, on_device(): pl.pallas_call(functools.partial(kernel, sections, owners), out_shape=jax...  33 us
    unnamed x1, local copies, waits for them, and re-layouts  2.26 us

profile of v3, /device:TPU:0, one launch (start us, length us, event | category | flops | bytes accessed | tf_op | source)
XLA Modules:
  0.0 35.3 jit_solution(10311084011166182971)
XLA Ops:
  0.0 33.0 %shard_map.73 = bf16[1,64,64,128]{3,2,1,0:T(8,128)(2,1)} custom-call(bf16[1,64,64,128]{3,2,1,0:T(8,128)(2,1)} %q_ref.1, bf16[1,64,4,128]{3,2,1,0:T(4,128)(2,1)} %sk_ref.1, bf16[1,64,4,128]{3,2,1,0:T(4,128)(2,1)} %sv_ref.1, bf16[1,32,4,128]{3,2,1,0:T(4,128)(2,1)} %ck_ref.1, bf16[1,32,4,128]{3,2,1,0:T(4,128)(2,1)} %cv_ref.1, s32[1,2,2,4]{3,2,1,0:T(2,128)} %bitcast.1, ...), custom_call_target="tpu_custom_call" | custom-call | tf_op jit(solution)/shard_map/pallas_call | solution.py:304
  33.0 2.3 %copy.9 = bf16[1,64,64,128]{3,2,1,0:T(8,128)(2,1)} copy(bf16[1,64,64,128]{3,2,1,0:T(8,128)(2,1)} %shard_map.73) | data formatting | bytes 2097152
